TPU v7x, 32 devices: a whole 2x2x4 slice. The times are simulated.
32 devices in a mesh: comp: 4 (over x, core), tx: 4 (over z), ty: 2 (over y).
Axes of the slice: x: 2, y: 2, z: 4, core: 2. Of those that a mesh axis runs over, the one named last changes fastest.
Arguments:
- model_state: float32 [4, 4, 8, 512, 512], P('comp', None, None, 'tx', 'ty'), may hold values from -6 to 6
- sea_mask: int32 [4, 512, 512], P('comp', 'tx', 'ty'), may hold values 0 or 1
- wave_speed: float32 [4, 8], P('comp'), may hold values from 0.1 to 0.4
- diffusivity: float32 [4, 8], P('comp'), may hold values from 0.02 to 0.2
- surface_gains: float32 [4, 3], P('comp'), may hold values from 0.1 to 0.5
- area_table: float32 [256], replicated, may hold values from 0.2 to 1
- own_cells: int32 [4, 8, 4, 2048], P('comp', ('tx', 'ty')), may hold values from 0 to 32767
- target_cells: int32 [4, 8, 4, 2048], P('comp', ('tx', 'ty')), may hold values from 0 to 32767
- weight_ids: int32 [4, 8, 4, 2048], P('comp', ('tx', 'ty')), may hold values from 0 to 255
- pair_counts: int32 [4, 8, 4], P('comp', ('tx', 'ty')), may hold values from 512 to 2048, as said below
- fold_map: int32 [512], replicated, may hold values from 0 to 511, as said below
Outputs:
- new_state: float32 [4, 4, 8, 512, 512], P('comp', None, None, 'tx', 'ty')
Inputs may be any that keep to these rules, and one draw needn't show every extreme that they name: pair_counts[g, s, n] counts the live slots that position s of component g sends to its partner n; in every component one receiving position gets 2048 from each of the positions that have it as a partner. fold_map[fold_map[x]] == x.
All inputs are finite; a program needn't handle non-finite values. No bound on the sum of `sea_mask` on one device may be relied on, other than what follows from the above.
Results may differ from a plain program's by a relative error of at most 0.0001.
Values sent between devices are 32-bit elements; how exact they have to be, the bound alone decides.
No kernel may reach another device: no remote copies, remote signals or barrier semaphores. Data moves between devices by JAX's collectives and lax.ppermute only.
A program may use at most 192 MiB of HBM per device.

v0:
```python
import jax
import jax.numpy as jnp
from jax import lax
from jax.sharding import PartitionSpec as P


def with_halo(array, sides, width):
    for axis, dim in sides:
        size, length = (lax.axis_size(axis), array.shape[dim])
        up = [(i, (i + 1) % size) for i in range(size)]
        down = [(j, i) for i, j in up]
        last = lax.slice_in_dim(array, length - width, length, axis=dim)
        first = lax.slice_in_dim(array, 0, width, axis=dim)
        before = lax.ppermute(last, axis, up)
        after = lax.ppermute(first, axis, down)
        array = jnp.concatenate([before, array, after], axis=dim)
    return array


def passed_along(block, axis, distance):
    devices = range(lax.axis_size(axis))
    route = [((i - distance) % len(devices), i) for i in devices]
    return lax.ppermute(block, axis, route)


def pick_cells(surface, cells, tile_rows, tile_cols):
    row_ids = jnp.arange(tile_rows, dtype=jnp.int32)
    col_ids = jnp.arange(tile_cols, dtype=jnp.int32)
    row_table = (cells[:, None] // tile_cols == row_ids[None, :]).astype(jnp.float32)
    col_table = (cells[:, None] % tile_cols == col_ids[None, :]).astype(jnp.float32)
    chosen_rows = jnp.einsum("kr,vrc->kvc", row_table, surface, precision=lax.Precision.HIGHEST)
    return jnp.einsum("kvc,kc->vk", chosen_rows, col_table, precision=lax.Precision.HIGHEST)


def add_cells(values, row_index, col_index, row_count, col_count):
    row_ids = jnp.arange(row_count, dtype=jnp.int32)
    col_ids = jnp.arange(col_count, dtype=jnp.int32)
    row_table = (row_index[:, None] == row_ids[None, :]).astype(jnp.float32)
    col_table = (col_index[:, None] == col_ids[None, :]).astype(jnp.float32)
    weighted = row_table[:, None, :] * jnp.transpose(values)[:, :, None]
    return jnp.einsum("kvr,kc->vrc", weighted, col_table, precision=lax.Precision.HIGHEST)


def extend_edges(fields, parity, fold_map, is_ocean):
    count_x = lax.axis_size("tx")
    count_y = lax.axis_size("ty")
    index_x = lax.axis_index("tx")
    index_y = lax.axis_index("ty")
    tile_rows = fields.shape[2]
    tile_cols = fields.shape[3]
    padded = with_halo(fields, (("tx", 2), ("ty", 3)), 1)
    atmosphere = jnp.logical_not(is_ocean)
    west_side = jnp.logical_and(atmosphere, index_x == 0)
    east_side = jnp.logical_and(atmosphere, index_x == count_x - 1)
    padded = padded.at[:, :, 0, :].multiply(jnp.where(west_side, 0.0, 1.0))
    padded = padded.at[:, :, tile_rows + 1, :].multiply(jnp.where(east_side, 0.0, 1.0))
    padded = padded.at[:, :, :, 0].multiply(jnp.where(index_y == 0, 0.0, 1.0))
    top_rows = fields[:, :, :, tile_cols - 1]
    whole_rows = lax.all_gather(top_rows, "tx", axis=2, tiled=True)
    partner = lax.dynamic_slice_in_dim(fold_map, index_x * tile_rows, tile_rows)
    folded = parity * jnp.take(whole_rows, partner, axis=2)
    northern = jnp.where(is_ocean, folded, jnp.zeros_like(folded))
    north_now = padded[:, :, 1 : tile_rows + 1, tile_cols + 1]
    chosen = jnp.where(index_y == count_y - 1, northern, north_now)
    return padded.at[:, :, 1 : tile_rows + 1, tile_cols + 1].set(chosen)


def shards(
    model_state,
    sea_mask,
    wave_speed,
    diffusivity,
    surface_gains,
    area_table,
    own_cells,
    target_cells,
    weight_ids,
    pair_counts,
    fold_map,
):
    comp_count = lax.axis_size("comp")
    row_step = lax.axis_size("ty")
    is_ocean = lax.axis_index("comp") == comp_count - 1
    fields = model_state[0]
    levels = fields.shape[1]
    tile_rows = fields.shape[2]
    tile_cols = fields.shape[3]
    sea_cells = sea_mask[0].astype(jnp.float32)
    near_count = own_cells.shape[2]
    slot_count = own_cells.shape[-1]
    slot_ids = jnp.arange(slot_count, dtype=jnp.int32)
    living = slot_ids[None, :] < pair_counts[0, 0][:, None]
    weight = jnp.where(living, area_table[weight_ids[0, 0]], 0.0)
    surface = fields[:, 0]
    picked = pick_cells(surface, own_cells[0, 0].reshape(-1), tile_rows, tile_cols).reshape(
        4, near_count, slot_count
    )
    slab = jnp.stack(
        [
            weight * picked[3],
            weight * picked[1],
            weight * picked[2],
            weight,
            target_cells[0, 0].astype(jnp.float32),
        ],
        axis=1,
    )
    arrived = [slab[0]]
    for partner in range(1, near_count):
        offset = partner % 2 + partner // 2 * row_step
        arrived.append(passed_along(slab[partner], ("tx", "ty"), offset))
    arrived = jnp.stack(arrived)
    receiver = jnp.where(is_ocean, slot_ids % (comp_count - 1), comp_count - 1)
    groups = jnp.arange(comp_count, dtype=jnp.int32)
    heading = (receiver[None, :] == groups[:, None])[:, None, None, :]
    routed = jnp.where(heading, arrived[None], 0.0)
    received = lax.all_to_all(routed, "comp", split_axis=0, concat_axis=0, tiled=True)

    def add_block(total, block):
        cells = block[:, 4].astype(jnp.int32).reshape(-1)
        values = jnp.moveaxis(block[:, :4], 1, 0).reshape(4, -1)
        return (
            total + add_cells(values, cells // tile_cols, cells % tile_cols, tile_rows, tile_cols),
            None,
        )

    start = jnp.zeros((4, tile_rows, tile_cols), jnp.float32)
    fluxes, unused = lax.scan(add_block, start, received)
    pressure, zonal, meridional, tracer = (fields[0], fields[1], fields[2], fields[3])
    first_level = (jnp.arange(levels, dtype=jnp.int32) == 0)[:, None, None]
    atmos_keep = jnp.where(first_level, 1.0 - surface_gains[0, 2] * (1.0 - sea_cells), 1.0)
    keeping = jnp.where(is_ocean, jnp.broadcast_to(sea_cells, atmos_keep.shape), atmos_keep)
    tendency_mask = jnp.where(is_ocean, sea_cells, 1.0)
    wave_factor = wave_speed[0][:, None, None]
    spread = diffusivity[0][:, None, None]
    scalars = extend_edges(jnp.stack([pressure, tracer]), 1.0, fold_map, is_ocean)
    pressure_pad, tracer_pad = (scalars[0], scalars[1])
    new_zonal = keeping * (
        zonal - 0.5 * wave_factor * (pressure_pad[:, 2:, 1:-1] - pressure_pad[:, :-2, 1:-1])
    )
    new_meridional = keeping * (
        meridional - 0.5 * wave_factor * (pressure_pad[:, 1:-1, 2:] - pressure_pad[:, 1:-1, :-2])
    )
    laplace = (
        tracer_pad[:, 2:, 1:-1]
        + tracer_pad[:, :-2, 1:-1]
        + tracer_pad[:, 1:-1, 2:]
        + tracer_pad[:, 1:-1, :-2]
        - 4.0 * tracer
    )
    new_tracer = tracer + spread * tendency_mask * laplace
    velocity = extend_edges(jnp.stack([new_zonal, new_meridional]), -1.0, fold_map, is_ocean)
    divergence = (
        velocity[0][:, 2:, 1:-1]
        - velocity[0][:, :-2, 1:-1]
        + velocity[1][:, 1:-1, 2:]
        - velocity[1][:, 1:-1, :-2]
    )
    new_pressure = pressure - 0.5 * wave_factor * divergence
    new_tracer = new_tracer.at[0].add(
        tendency_mask * surface_gains[0, 0] * (fluxes[0] - fluxes[3] * tracer[0])
    )
    new_zonal = new_zonal.at[0].add(
        tendency_mask * surface_gains[0, 1] * (fluxes[1] - fluxes[3] * zonal[0])
    )
    new_meridional = new_meridional.at[0].add(
        tendency_mask * surface_gains[0, 1] * (fluxes[2] - fluxes[3] * meridional[0])
    )
    return jnp.stack([new_pressure, new_zonal, new_meridional, new_tracer])[None]


def solution(mesh):
    in_specs = (
        P("comp", None, None, "tx", "ty"),
        P("comp", "tx", "ty"),
        P("comp", None),
        P("comp", None),
        P("comp", None),
        P(),
        P("comp", ("tx", "ty"), None, None),
        P("comp", ("tx", "ty"), None, None),
        P("comp", ("tx", "ty"), None, None),
        P("comp", ("tx", "ty"), None),
        P(),
    )
    out_specs = P("comp", None, None, "tx", "ty")
    return jax.shard_map(shards, mesh=mesh, in_specs=in_specs, out_specs=out_specs, check_vma=False)
```

profile of v0, /device:TPU:3, one launch (start us, length us, event | category | flops | bytes accessed | tf_op | source)
XLA Modules:
  0.0 819.7 jit_solution(463393753076584609)
XLA Ops:
  0.0 1.8 slice_bitcast_fusion.1
  1.8 0.8 copy.353
  2.6 3.3 collective-permute-start.1
  6.0 0.8 copy.352
  6.8 4.7 copy.424
  11.5 0.8 copy.415
  12.2 0.8 fusion.64
  13.0 51.2 %gather_fusion = f32[8192]{0:T(1024)S(1)} fusion(f32[256]{0:T(256)S(1)} %copy-done, s32[8192]{0:T(1024)S(1)} %broadcast_clamp_fusion), kind=kCustom, calls=%fused_computation.2 | custom fusion | bytes 98304 | tf_op jit(solution)/shard_map/gather | solution.py:93
  64.3 1.4 fusion.19
  65.7 18.2 %fusion.21 = f32[8192,4,256]{2,0,1:T(8,128)} fusion(s32[8192]{0:T(1024)S(1)} %get-tuple-element.234, f32[4,8,128,256]{3,2,0,1:T(8,128)} %bitcast.200), kind=kOutput, calls=%fused_computation.36 | convolution fusion | flops 12885950464 | bytes 34111488 | tf_op jit(solution)/shard_map/kr,vrc->kvc/dot_general | solution.py:31
  84.0 87.8 %fusion.16 = f32[8192,1,4]{2,1,0:T(1,128)} fusion(f32[8192,4,256]{2,0,1:T(8,128)} %fusion.21, pred[8192,256,1]{1,0,2:T(32,128)(4,1)S(1)} %fusion.19), kind=kOutput, calls=%fused_computation.27 | convolution fusion | flops 100663296 | bytes 35782656 | tf_op jit(solution)/shard_map/kvc,kc->vk/dot_general | solution.py:32
  171.8 7.9 copy.393
  182.4 1.7 collective-permute-start.10
  184.8 3.0 collective-permute-start.8
  190.0 1.5 pad_maximum_fusion.2
  192.8 0.8 compare_and_fusion
  194.3 1.2 multiply_subtract_fusion
  195.9 26.0 %copy.354 = f32[2,8,128,256]{1,0,2,3:T(2,128)} copy(f32[2,8,128,256]{3,2,1,0:T(8,128)} %pad_maximum_fusion.2) | data formatting | bytes 4194304 | tf_op jit(solution)/shard_map/stack | solution.py:136
  221.8 1.1 pad_maximum_fusion.10
  223.2 1.3 collective-permute-start.3
  224.7 10.2 %all-gather = f32[2,8,512,1]{2,1,3,0:T(8,128)S(1)} all-gather(f32[2,8,128,1]{2,1,3,0:T(8,128)S(1)} %copy.407), channel_id=2, replica_groups=mesh['comp'=4,'tx'=4,'ty'=2] {'tx'}, dimensions={2}, use_global_device_ids=true | all-gather | bytes 40960 | tf_op jit(solution)/shard_map/all_gather | solution.py:59
  236.8 116.2 %pad_maximum_fusion = f32[2,8,130,258]{1,0,2,3:T(2,128)} fusion(f32[2,8,130,1]{1,0,2,3:T(2,128)S(1)} %copy.358, f32[2,8,1,256]{1,0,2,3:T(2,128)S(1)} %collective-permute-done.1, f32[2,8,128,256]{1,0,2,3:T(2,128)} %copy.354, f32[2,8,1,256]{1,0,2,3:T(2,128)} %collective-permute-done, f32[2,8,130,1]{1,0,2,3:T(2,128)S(1)} %copy.357), kind=kLoop, calls=%fused_computation.25 | loop fusion | flops 2146560 | bytes 4293120 | tf_op jit(solution)/shard_map/concatenate | solution.py:16
  353.1 1.8 fusion.41
  354.9 1.9 fusion.40
  356.7 1.6 fusion.43
  358.3 1.8 fusion.55
  360.1 34.6 %fusion.77 = (f32[1,8,130,258]{1,0,2,3:T(1,128)}, f32[1,8,130,258]{1,0,2,3:T(1,128)}) fusion(f32[2,8,130,258]{1,0,2,3:T(2,128)} %fusion.55), kind=kLoop, calls=%fused_computation.173 | loop fusion | bytes 4293120 | tf_op jit(solution)/shard_map/slice | solution.py:137
  394.7 32.4 %copy.394 = f32[1,8,130,258]{3,2,1,0:T(8,128)} copy(f32[1,8,130,258]{1,0,2,3:T(1,128)} %get-tuple-element.210) | data formatting | bytes 2146560 | tf_op jit(solution)/shard_map/squeeze | solution.py:137
  427.1 4.7 fusion.37
  432.2 1.5 pad_maximum_fusion.3
  433.7 1.0 copy.452
  434.7 1.0 copy.450
  435.7 0.8 copy.366
  436.5 0.8 copy.367
  437.5 1.4 collective-permute-start.4
  439.2 13.0 %all-gather.1 = f32[2,8,512,1]{2,1,3,0:T(8,128)S(1)} all-gather(f32[2,8,128,1]{2,1,3,0:T(8,128)S(1)} %copy.408), channel_id=3, replica_groups=mesh['comp'=4,'tx'=4,'ty'=2] {'tx'}, dimensions={2}, use_global_device_ids=true | all-gather | bytes 40960 | tf_op jit(solution)/shard_map/all_gather | solution.py:59
  453.1 32.6 %copy.402 = f32[1,8,130,258]{3,2,1,0:T(8,128)} copy(f32[1,8,130,258]{1,0,2,3:T(1,128)} %get-tuple-element.211) | data formatting | bytes 2146560 | tf_op jit(solution)/shard_map/squeeze | solution.py:137
  485.7 26.0 %copy.368 = f32[2,8,128,256]{1,0,2,3:T(2,128)} copy(f32[2,8,128,256]{3,2,1,0:T(8,128)} %pad_maximum_fusion.3) | data formatting | bytes 4194304 | tf_op jit(solution)/shard_map/stack | solution.py:152
  511.7 0.9 pad_maximum_fusion.4
  512.8 1.1 pad_maximum_fusion.7
  514.2 1.6 collective-permute-start.7
  515.9 1.0 broadcast_select_fusion
  516.9 12.2 %all-to-all-start = ((f32[4,4,5,2048]{3,1,2,0:T(4,128)}), f32[4,4,5,2048]{3,1,2,0:T(4,128)}, u32[]{:S(2)}, u32[]{:S(2)}) async-start(f32[4,4,5,2048]{3,1,2,0:T(4,128)} %broadcast_select_fusion), calls=%async_computation | async-start | bytes 1310720 | tf_op jit(solution)/shard_map/all_to_all | solution.py:117
  529.4 116.2 %pad_maximum_fusion.1 = f32[2,8,130,258]{1,0,2,3:T(2,128)} fusion(f32[2,8,130,1]{1,0,2,3:T(2,128)S(1)} %copy.372, f32[2,8,1,256]{1,0,2,3:T(2,128)S(1)} %collective-permute-done.5, f32[2,8,128,256]{1,0,2,3:T(2,128)} %copy.368, f32[2,8,1,256]{1,0,2,3:T(2,128)} %collective-permute-done.4, f32[2,8,130,1]{1,0,2,3:T(2,128)S(1)} %copy.371), kind=kLoop, calls=%fused_computation.26 | loop fusion | flops 2146560 | bytes 4293120 | tf_op jit(solution)/shard_map/concatenate | solution.py:16
  645.6 1.8 fusion.39
  647.4 1.9 fusion.38
  649.2 1.6 fusion.42
  650.8 1.8 fusion.52
  652.6 34.6 %fusion.76 = (f32[1,8,130,258]{1,0,2,3:T(1,128)}, f32[1,8,130,258]{1,0,2,3:T(1,128)}) fusion(f32[2,8,130,258]{1,0,2,3:T(2,128)} %fusion.52), kind=kLoop, calls=%fused_computation.172 | loop fusion | bytes 4293120 | tf_op jit(solution)/shard_map/slice | solution.py:154
  687.2 32.4 %copy.398 = f32[1,8,130,258]{3,2,1,0:T(8,128)} copy(f32[1,8,130,258]{1,0,2,3:T(1,128)} %get-tuple-element.208) | data formatting | bytes 2146560 | tf_op jit(solution)/shard_map/squeeze | solution.py:154
  719.5 32.3 %copy.400 = f32[1,8,130,258]{3,2,1,0:T(8,128)} copy(f32[1,8,130,258]{1,0,2,3:T(1,128)} %get-tuple-element.209) | data formatting | bytes 2146560 | tf_op jit(solution)/shard_map/squeeze | solution.py:156
  751.8 8.5 %fusion.31 = (f32[1,8,128,256]{3,2,1,0:T(8,128)}, f32[8,128,256]{2,1,0:T(8,128)S(1)}) fusion(f32[8,130,258]{2,1,0:T(8,128)} %bitcast.199, f32[8,130,258]{2,1,0:T(8,128)} %bitcast.198, f32[1,4,8,128,256]{4,3,2,1,0:T(8,128)} %param.37, f32[8]{0:T(128)S(1)} %copy-done.12, f32[8,130,258]{2,1,0:T(8,128)} %bitcast.196, f32[128,256]{1,0:T(8,128)S(1)} %copy-done.4, ...), kind=kLoop, calls=%fused_computation.63 | loop fusion | flops 3407872 | bytes 12714048 | tf_op jit(solution)/shard_map/stack | solution.py:169
  760.3 1.0 copy.451
  761.3 50.0 %while.24 = (s32[]{:T(128)}, f32[4,128,256]{2,1,0:T(8,128)}, f32[4,4,5,2048]{3,1,2,0:T(4,128)}, s32[]{:T(128)}, s32[]{:T(128)}) while((s32[]{:T(128)}, f32[4,128,256]{2,1,0:T(8,128)}, f32[4,4,5,2048]{3,1,2,0:T(4,128)}, s32[]{:T(128)}, s32[]{:T(128)}) %tuple.98), condition=%wide.region_1.3_spmd.clone, body=%wide.region_0.2_spmd.clone.sunk | while | flops 12893716480 | bytes 10715219 | solution.py:128
  761.5 0.9 dynamic-slice_bitcast_fusion.2
  763.1 10.1 %fusion.89 = f32[4,128,256]{2,1,0:T(8,128)} fusion(s32[8192]{0:T(1024)S(1)} %get-tuple-element.259, f32[8192,4]{0,1:T(4,128)S(1)} %bitcast.203, f32[8192,128]{0,1:T(8,128)S(1)} %fusion.88, f32[4,128,256]{2,1,0:T(8,128)} %get-tuple-element.267, pred[]{:T(512)S(6)} %compare.86), kind=kOutput, calls=%fused_computation.12.clone.1 | convolution fusion | flops 12891455488 | bytes 5406721 | tf_op jit(solution)/shard_map/while/body/eval_jaxpr/kvr,kc->vrc/dot_general | solution.py:41
  773.2 0.9 dynamic-slice_bitcast_fusion.2
  774.8 11.1 %fusion.89 = f32[4,128,256]{2,1,0:T(8,128)} fusion(s32[8192]{0:T(1024)S(1)} %get-tuple-element.259, f32[8192,4]{0,1:T(4,128)S(1)} %bitcast.203, f32[8192,128]{0,1:T(8,128)S(1)} %fusion.88, f32[4,128,256]{2,1,0:T(8,128)} %get-tuple-element.267, pred[]{:T(512)S(6)} %compare.86), kind=kOutput, calls=%fused_computation.12.clone.1 | convolution fusion | flops 12891455488 | bytes 5406721 | tf_op jit(solution)/shard_map/while/body/eval_jaxpr/kvr,kc->vrc/dot_general | solution.py:41
  785.9 0.9 dynamic-slice_bitcast_fusion.2
  787.5 11.1 %fusion.89 = f32[4,128,256]{2,1,0:T(8,128)} fusion(s32[8192]{0:T(1024)S(1)} %get-tuple-element.259, f32[8192,4]{0,1:T(4,128)S(1)} %bitcast.203, f32[8192,128]{0,1:T(8,128)S(1)} %fusion.88, f32[4,128,256]{2,1,0:T(8,128)} %get-tuple-element.267, pred[]{:T(512)S(6)} %compare.86), kind=kOutput, calls=%fused_computation.12.clone.1 | convolution fusion | flops 12891455488 | bytes 5406721 | tf_op jit(solution)/shard_map/while/body/eval_jaxpr/kvr,kc->vrc/dot_general | solution.py:41
  798.6 0.9 dynamic-slice_bitcast_fusion.2
  800.2 11.1 %fusion.89 = f32[4,128,256]{2,1,0:T(8,128)} fusion(s32[8192]{0:T(1024)S(1)} %get-tuple-element.259, f32[8192,4]{0,1:T(4,128)S(1)} %bitcast.203, f32[8192,128]{0,1:T(8,128)S(1)} %fusion.88, f32[4,128,256]{2,1,0:T(8,128)} %get-tuple-element.267, pred[]{:T(512)S(6)} %compare.86), kind=kOutput, calls=%fused_computation.12.clone.1 | convolution fusion | flops 12891455488 | bytes 5406721 | tf_op jit(solution)/shard_map/while/body/eval_jaxpr/kvr,kc->vrc/dot_general | solution.py:41
  811.3 3.3 fusion.49
  814.6 4.6 maximum_bitcast_fusion
  (117 shorter events, 15.0 us)
Async XLA Ops:
  0.0 13.0 %copy-start = (f32[256]{0:T(256)S(1)}, f32[256]{0:T(256)}, u32[]{:S(2)}) copy-start(f32[256]{0:T(256)} %param.42) | copy-start | bytes 3076
  2.6 219.2 %collective-permute-start.1 = (f32[2,8,1,256]{1,0,2,3:T(2,128)}, f32[2,8,1,256]{1,0,2,3:T(2,128)S(1)}, u32[]{:S(2)}, u32[]{:S(2)}) collective-permute-start(f32[2,8,1,256]{1,0,2,3:T(2,128)} %copy.353), channel_id=1, source_target_pairs={{2,0},{4,2},{6,4},{0,6},{3,1},{5,3},{7,5},{1,7},{10,8},{12,10},{14... | collective-permute-start | bytes 49160 | tf_op jit(solution)/shard_map/ppermute | solution.py:15
  6.8 215.0 %collective-permute-start = (f32[2,8,1,256]{1,0,2,3:T(2,128)}, f32[2,8,1,256]{1,0,2,3:T(2,128)}, u32[]{:S(2)}, u32[]{:S(2)}) collective-permute-start(f32[2,8,1,256]{1,0,2,3:T(2,128)} %copy.352), channel_id=1, source_target_pairs={{0,2},{2,4},{4,6},{6,0},{1,3},{3,5},{5,7},{7,1},{8,10},{10,12},{12... | collective-permute-start | bytes 49160 | tf_op jit(solution)/shard_map/ppermute | solution.py:14
  84.0 96.1 %copy-start.10 = (s32[1,1,4]{2,1,0:T(1,128)S(1)}, s32[1,1,4]{2,1,0:T(1,128)}, u32[]{:S(2)}) copy-start(s32[1,1,4]{2,1,0:T(1,128)} %param.46) | copy-start | bytes 52
  84.0 96.5 %copy-start.9 = (s32[1,1,4,2048]{3,2,1,0:T(4,128)S(1)}, s32[1,1,4,2048]{3,2,1,0:T(4,128)}, u32[]{:S(2)}) copy-start(s32[1,1,4,2048]{3,2,1,0:T(4,128)} %param.44) | copy-start | bytes 98308
  84.0 104.4 %copy-start.2 = (s32[1,128,256]{2,1,0:T(8,128)S(1)}, s32[1,128,256]{2,1,0:T(8,128)}, u32[]{:S(2)}) copy-start(s32[1,128,256]{2,1,0:T(8,128)} %param.38) | copy-start | bytes 393220
  84.0 107.6 %copy-start.14 = (f32[1,8]{1,0:T(1,128)S(1)}, f32[1,8]{1,0:T(1,128)}, u32[]{:S(2)}) copy-start(f32[1,8]{1,0:T(1,128)} %param.39) | copy-start | bytes 100
  84.0 108.2 %copy-start.11 = (f32[1,3]{1,0:T(1,128)S(1)}, f32[1,3]{1,0:T(1,128)}, u32[]{:S(2)}) copy-start(f32[1,3]{1,0:T(1,128)} %param.41) | copy-start | bytes 40
  181.8 329.9 %collective-permute-start.9 = (f32[5,2048]{1,0:T(8,128)}, f32[5,2048]{1,0:T(8,128)}, u32[]{:S(2)}, u32[]{:S(2)}) collective-permute-start(f32[5,2048]{1,0:T(8,128)} %bitcast.173), channel_id=1, source_target_pairs={{6,0},{7,1},{0,2},{1,3},{2,4},{3,5},{4,6},{5,7},{14,8},{15,9},{8,1... | collective-permute-start | bytes 122888 | tf_op jit(solution)/shard_map/ppermute | solution.py:23
  182.4 329.3 %collective-permute-start.10 = (f32[5,2048]{1,0:T(8,128)}, f32[5,2048]{1,0:T(8,128)}, u32[]{:S(2)}, u32[]{:S(2)}) collective-permute-start(f32[5,2048]{1,0:T(8,128)} %bitcast.175), channel_id=1, source_target_pairs={{5,0},{6,1},{7,2},{0,3},{1,4},{2,5},{3,6},{4,7},{13,8},{14,9},{15,... | collective-permute-start | bytes 122888 | tf_op jit(solution)/shard_map/ppermute | solution.py:23
  184.8 327.0 %collective-permute-start.8 = (f32[5,2048]{1,0:T(8,128)}, f32[5,2048]{1,0:T(8,128)}, u32[]{:S(2)}, u32[]{:S(2)}) collective-permute-start(f32[5,2048]{1,0:T(8,128)} %bitcast.174), channel_id=1, source_target_pairs={{7,0},{0,1},{1,2},{2,3},{3,4},{4,5},{5,6},{6,7},{15,8},{8,9},{9,10... | collective-permute-start | bytes 122888 | tf_op jit(solution)/shard_map/ppermute | solution.py:23
  221.8 13.3 %copy-start.8 = (f32[1,5,2048]{2,0,1:T(1,128)S(1)}, f32[1,5,2048]{2,0,1:T(1,128)}, u32[]{:S(2)}) copy-start(f32[1,5,2048]{2,0,1:T(1,128)} %get-tuple-element.229) | copy-start | bytes 122884
  223.2 13.5 %collective-permute-start.3 = (f32[2,8,130,1]{2,1,3,0:T(8,128)S(1)}, f32[2,8,130,1]{2,1,3,0:T(8,128)S(1)}, u32[]{:S(2)}, u32[]{:S(2)}) collective-permute-start(f32[2,8,130,1]{2,1,3,0:T(8,128)S(1)} %copy.356), channel_id=1, source_target_pairs={{1,0},{0,1},{3,2},{2,3},{5,4},{4,5},{7,6},{6,7},{9,8},{8,9},{11,10... | collective-permute-start | bytes 24968 | tf_op jit(solution)/shard_map/ppermute | solution.py:15
  224.5 12.1 %collective-permute-start.2 = (f32[2,8,130,1]{2,1,3,0:T(8,128)S(1)}, f32[2,8,130,1]{2,1,3,0:T(8,128)S(1)}, u32[]{:S(2)}, u32[]{:S(2)}) collective-permute-start(f32[2,8,130,1]{2,1,3,0:T(8,128)S(1)} %copy.355), channel_id=1, source_target_pairs={{0,1},{1,0},{2,3},{3,2},{4,5},{5,4},{6,7},{7,6},{8,9},{9,8},{10,11... | collective-permute-start | bytes 24968 | tf_op jit(solution)/shard_map/ppermute | solution.py:14
  394.7 32.4 %copy-start.5 = (f32[128,256]{1,0:T(8,128)S(1)}, f32[128,256]{1,0:T(8,128)}, u32[]{:S(2)}) copy-start(f32[128,256]{1,0:T(8,128)} %convert_bitcast_fusion) | copy-start | bytes 393220
  394.7 32.4 %copy-start.6 = (f32[128,256]{1,0:T(8,128)S(1)}, f32[128,256]{1,0:T(8,128)}, u32[]{:S(2)}) copy-start(f32[128,256]{1,0:T(8,128)} %multiply_subtract_fusion) | copy-start | bytes 393220
  394.7 32.4 %copy-start.12 = (f32[8]{0:T(128)S(1)}, f32[8]{0:T(128)}, u32[]{:S(2)}) copy-start(f32[8]{0:T(128)} %multiply_bitcast_fusion) | copy-start | bytes 100
  437.4 75.4 %collective-permute-start.5 = (f32[2,8,1,256]{1,0,2,3:T(2,128)}, f32[2,8,1,256]{1,0,2,3:T(2,128)S(1)}, u32[]{:S(2)}, u32[]{:S(2)}) collective-permute-start(f32[2,8,1,256]{1,0,2,3:T(2,128)} %copy.367), channel_id=1, source_target_pairs={{2,0},{4,2},{6,4},{0,6},{3,1},{5,3},{7,5},{1,7},{10,8},{12,10},{14... | collective-permute-start | bytes 49160 | tf_op jit(solution)/shard_map/ppermute | solution.py:15
  437.5 75.3 %collective-permute-start.4 = (f32[2,8,1,256]{1,0,2,3:T(2,128)}, f32[2,8,1,256]{1,0,2,3:T(2,128)}, u32[]{:S(2)}, u32[]{:S(2)}) collective-permute-start(f32[2,8,1,256]{1,0,2,3:T(2,128)} %copy.366), channel_id=1, source_target_pairs={{0,2},{2,4},{4,6},{6,0},{1,3},{3,5},{5,7},{7,1},{8,10},{10,12},{12... | collective-permute-start | bytes 49160 | tf_op jit(solution)/shard_map/ppermute | solution.py:14
  485.7 26.0 %copy-start.7 = (f32[1,5,2048]{2,1,0:T(8,128)S(1)}, f32[1,5,2048]{2,1,0:T(8,128)}, u32[]{:S(2)}) copy-start(f32[1,5,2048]{2,1,0:T(8,128)} %copy.409) | copy-start | bytes 122884
  514.2 15.0 %collective-permute-start.7 = (f32[2,8,130,1]{2,1,3,0:T(8,128)S(1)}, f32[2,8,130,1]{2,1,3,0:T(8,128)S(1)}, u32[]{:S(2)}, u32[]{:S(2)}) collective-permute-start(f32[2,8,130,1]{2,1,3,0:T(8,128)S(1)} %copy.370), channel_id=1, source_target_pairs={{1,0},{0,1},{3,2},{2,3},{5,4},{4,5},{7,6},{6,7},{9,8},{8,9},{11,10... | collective-permute-start | bytes 24968 | tf_op jit(solution)/shard_map/ppermute | solution.py:15
  515.8 13.3 %collective-permute-start.6 = (f32[2,8,130,1]{2,1,3,0:T(8,128)S(1)}, f32[2,8,130,1]{2,1,3,0:T(8,128)S(1)}, u32[]{:S(2)}, u32[]{:S(2)}) collective-permute-start(f32[2,8,130,1]{2,1,3,0:T(8,128)S(1)} %copy.369), channel_id=1, source_target_pairs={{0,1},{1,0},{2,3},{3,2},{4,5},{5,4},{6,7},{7,6},{8,9},{9,8},{10,11... | collective-permute-start | bytes 24968 | tf_op jit(solution)/shard_map/ppermute | solution.py:14
  516.9 244.4 %all-to-all-start = ((f32[4,4,5,2048]{3,1,2,0:T(4,128)}), f32[4,4,5,2048]{3,1,2,0:T(4,128)}, u32[]{:S(2)}, u32[]{:S(2)}) async-start(f32[4,4,5,2048]{3,1,2,0:T(4,128)} %broadcast_select_fusion), calls=%async_computation | async-start | bytes 1310720 | tf_op jit(solution)/shard_map/all_to_all | solution.py:117
  687.2 64.7 %copy-start.4 = (f32[128,256]{1,0:T(8,128)S(1)}, f32[128,256]{1,0:T(8,128)}, u32[]{:S(2)}) copy-start(f32[128,256]{1,0:T(8,128)} %fusion.63) | copy-start | bytes 393220
  687.2 64.7 %copy-start.13 = (f32[1,8]{1,0:T(1,128)S(1)}, f32[1,8]{1,0:T(1,128)}, u32[]{:S(2)}) copy-start(f32[1,8]{1,0:T(1,128)} %param.40) | copy-start | bytes 100
  761.3 50.0 %copy-start.3 = (s32[1,128,256]{2,1,0:T(8,128)S(1)}, s32[1,128,256]{2,1,0:T(8,128)}, u32[]{:S(2)}) copy-start(s32[1,128,256]{2,1,0:T(8,128)} %param.38) | copy-start | bytes 393220
  811.3 8.0 copy-start.1
where the time goes:
time: 833 us; the launch traced here: 820 us
  local copies, waits for them, and re-layouts  335 us (40%)
  other arithmetic  285 us (34%)
  matrix products  150 us (18%)
  starting transfers between devices  24.9 us (3%)
  blocking collectives  23.2 us (3%)
    concatenate x2, other arithmetic, with_halo(): array = jnp.concatenate([before, array, after], axis=dim)  232 us
    dot_general x1, matrix products, pick_cells(): jnp.einsum('kvc,kc->vk', chosen_rows, col_table, precision=lax.Precision....  87.8 us
    squeeze x2, local copies, waits for them, and re-layouts, shards(): pressure_pad, tracer_pad = (scalars[0], scalars[1])  65 us
    gather x2, local copies, waits for them, and re-layouts, shards(): weight = jnp.where(living, area_table[weight_ids[0, 0]], 0.0)  51.2 us
    dot_general x4, matrix products, add_cells(): jnp.einsum('kvr,kc->vrc', weighted, col_table, precision=lax.Precision.HI...  43.6 us
    slice x1, local copies, waits for them, and re-layouts, shards(): pressure_pad, tracer_pad = (scalars[0], scalars[1])  34.6 us
    slice x1, local copies, waits for them, and re-layouts, shards(): velocity[0][:, 2:, 1:-1] - velocity[0][:, :-2, 1:-1]  34.6 us
    squeeze x1, local copies, waits for them, and re-layouts, shards(): velocity[0][:, 2:, 1:-1] - velocity[0][:, :-2, 1:-1]  32.4 us
  transfers between devices with their start and end apart: 12, of which 0 were waited for; matrix products, arithmetic and copies ran while one was open for 86% of the time, Pallas kernels for 0%

commit v1 on v0

v1 whole, which is shorter than its diff:
```python
import functools

import jax
import jax.numpy as jnp
from jax import lax
from jax.experimental import pallas as pl
from jax.experimental.pallas import tpu as pltpu
from jax.sharding import PartitionSpec as P

LANES = 128
VMEM_BYTES = 56 * 1024 * 1024
F32 = jnp.float32
BF16 = jnp.bfloat16
I32 = jnp.int32

EDGE_P, SECOND_P, EDGE_VELOCITY, EDGE_T = range(4)
CHANNELS = 5


def split_two(values):
    high = values.astype(BF16)
    low = (values - high.astype(F32)).astype(BF16)
    return high, low


def iota(shape, dim):
    return lax.broadcasted_iota(I32, shape, dim)


def halo_rows(levels):
    return (4 * levels + 1 + 7) // 8 * 8


def pack_body(levels, rows, cols, y_pair, state_ref, mask_ref, up_ref, down_ref, *y_refs):
    level = pl.program_id(0)
    height = halo_rows(levels)
    pressure, zonal, meridional, tracer = (state_ref[0, v, 0] for v in range(4))
    lane = iota((rows, LANES), 1)

    def put_rows(ref, row, values):
        for part in range(cols // LANES):
            ref[pl.ds(part * height + row, 1), :] = values[:, part * LANES : (part + 1) * LANES]

    def row_of(field, at):
        return field[at : at + 1, :]

    for ref, edge, second in ((up_ref, rows - 1, rows - 2), (down_ref, 0, 1)):
        put_rows(ref, EDGE_P * levels + level, row_of(pressure, edge))
        put_rows(ref, SECOND_P * levels + level, row_of(pressure, second))
        put_rows(ref, EDGE_VELOCITY * levels + level, row_of(zonal, edge))
        put_rows(ref, EDGE_T * levels + level, row_of(tracer, edge))

    def columns(field_list):
        picked = []
        for field, at in field_list:
            picked.append(jnp.broadcast_to(field[:, at : at + 1], (rows, LANES)))
        return picked

    high = columns(((pressure, cols - 1), (pressure, cols - 2), (meridional, cols - 1), (tracer, cols - 1)))
    low = columns(((pressure, 0), (pressure, 1), (meridional, 0), (tracer, 0)))

    def put_columns(ref, start, values):
        block = ref[pl.ds(start, rows), :]
        for q in range(4):
            block = jnp.where(lane == q * levels + level, values[q], block)
        ref[pl.ds(start, rows), :] = block

    fold_start = height * (cols // LANES)

    @pl.when(level == 0)
    def _():
        sea = mask_ref[0].astype(F32)
        at = 4 * levels
        for ref, edge in ((up_ref, rows - 1), (down_ref, 0)):
            for part in range(cols // LANES):
                ref[part * height + at : (part + 1) * height, :] = jnp.zeros((height - at, LANES), F32)
            put_rows(ref, at, row_of(sea, edge))
        sea_high = jnp.where(lane == at, jnp.broadcast_to(sea[:, cols - 1 : cols], (rows, LANES)), 0.0)
        sea_low = jnp.where(lane == at, jnp.broadcast_to(sea[:, 0:1], (rows, LANES)), 0.0)
        up_ref[fold_start : fold_start + rows, :] = sea_high
        if y_pair:
            first = lax.axis_index("ty") == 0
            y_refs[0][...] = jnp.where(first, sea_high, sea_low)
        else:
            y_refs[0][...] = sea_low

    put_columns(up_ref, fold_start, high)
    if y_pair:
        first = lax.axis_index("ty") == 0
        put_columns(y_refs[0], 0, [jnp.where(first, h, lo) for h, lo in zip(high, low)])
    else:
        put_columns(y_refs[0], 0, low)

    @pl.when(level == levels - 1)
    def _():
        down_ref[fold_start : fold_start + rows, :] = up_ref[fold_start : fold_start + rows, :]


def pack_halos(model_state, sea_mask, y_pair):
    levels, rows, cols = model_state.shape[2:]
    height = halo_rows(levels) * (cols // LANES)
    tall = jax.ShapeDtypeStruct((height + rows, LANES), F32)
    whole = lambda shape: pl.BlockSpec(shape, lambda l: (0,) * len(shape))
    return pl.pallas_call(
        functools.partial(pack_body, levels, rows, cols, y_pair),
        grid=(levels,),
        in_specs=[
            pl.BlockSpec((1, 4, 1, rows, cols), lambda l: (0, 0, l, 0, 0)),
            whole((1, rows, cols)),
        ],
        out_specs=[whole((height + rows, LANES))] * 2 + [whole((rows, LANES))],
        out_shape=[tall, tall, jax.ShapeDtypeStruct((rows, LANES), F32)],
        compiler_params=pltpu.CompilerParams(vmem_limit_bytes=VMEM_BYTES),
    )(model_state, sea_mask)


def gather_body(rows, cols, slots, state_ref, own_ref, target_ref, ids_ref, table_ref, counts_ref, *rest):
    out_refs, fields_ref = rest[:-1], rest[-1]
    near = own_ref.shape[2]
    for v in range(3):
        high, low = split_two(state_ref[0, v + 1, 0])
        fields_ref[v * rows : (v + 1) * rows, :] = high
        fields_ref[(v + 3) * rows : (v + 4) * rows, :] = low
    step = 512
    tables = [
        jnp.broadcast_to(table_ref[t : t + 1, :], (8, LANES)) for t in range(table_ref.shape[0])
    ]
    col_ids = iota((cols, step), 0)
    row_ids = iota((rows, step), 0)
    lane = iota((1, LANES), 1)
    for n in range(near):
        count = counts_ref[0, 0, n]

        def one(c, carry, n=n, count=count):
            start = pl.multiple_of(c * step, step)
            cells = own_ref[0, 0, n : n + 1, pl.ds(start, step)]
            picks = (col_ids == cells % cols).astype(F32).astype(BF16)
            found = jnp.dot(fields_ref[...], picks, preferred_element_type=F32)
            in_row = row_ids == cells // cols
            values = []
            for v in range(3):
                both = found[v * rows : (v + 1) * rows] + found[(v + 3) * rows : (v + 4) * rows]
                values.append(jnp.sum(jnp.where(in_row, both, 0.0), axis=0, keepdims=True))
            for part in range(step // LANES):
                at = c * (step // LANES) + part
                here = pl.multiple_of(start + part * LANES, LANES)
                ids = jnp.broadcast_to(ids_ref[0, 0, n : n + 1, pl.ds(here, LANES)], (8, LANES))
                weight = jnp.zeros((8, LANES), F32)
                for t, table in enumerate(tables):
                    looked = jnp.take_along_axis(table, ids % LANES, axis=1)
                    weight = jnp.where(ids // LANES == t, looked, weight)
                weight = jnp.where(here + lane < count, weight[:1], 0.0)
                cut = slice(part * LANES, (part + 1) * LANES)
                out = out_refs[n]
                out[0, pl.ds(at, 1), :] = weight * values[2][:, cut]
                out[1, pl.ds(at, 1), :] = weight * values[0][:, cut]
                out[2, pl.ds(at, 1), :] = weight * values[1][:, cut]
                out[3, pl.ds(at, 1), :] = weight
                out[4, pl.ds(at, 1), :] = target_ref[0, 0, n : n + 1, pl.ds(here, LANES)].astype(F32)
            return carry

        lax.fori_loop(0, slots // step, one, 0)


def gather_slots(model_state, own_cells, target_cells, weight_ids, area_table, pair_counts):
    rows, cols = model_state.shape[3:]
    near, slots = own_cells.shape[2:]
    table = area_table.reshape(-1, LANES)
    whole = lambda shape: pl.BlockSpec(shape, lambda i: (0,) * len(shape))
    slab = (CHANNELS, slots // LANES, LANES)
    return pl.pallas_call(
        functools.partial(gather_body, rows, cols, slots),
        grid=(1,),
        in_specs=[
            whole((1, 4, 1, rows, cols)),
            whole(own_cells.shape),
            whole(target_cells.shape),
            whole(weight_ids.shape),
            whole(table.shape),
            pl.BlockSpec(memory_space=pltpu.SMEM),
        ],
        out_specs=[whole(slab)] * near,
        out_shape=[jax.ShapeDtypeStruct(slab, F32)] * near,
        scratch_shapes=[pltpu.VMEM((6 * rows, cols), BF16)],
        compiler_params=pltpu.CompilerParams(vmem_limit_bytes=VMEM_BYTES),
    )(model_state, own_cells, target_cells, weight_ids, table, pair_counts)


def stencil_body(
    levels, rows, cols, comps, count_x, count_y,
    state_ref, mask_ref, west_ref, east_ref, south_ref, north_ref, own_ref, fold_ref,
    wave_ref, spread_ref, gains_ref, *rest,
):
    far_refs, out_ref, turned_ref = rest[:-2], rest[-2], rest[-1]
    level = pl.program_id(0)
    height = halo_rows(levels)
    fold_start = height * (cols // LANES)
    index_x = lax.axis_index("tx")
    index_y = lax.axis_index("ty")
    is_ocean = lax.axis_index("comp") == comps - 1
    last_y = index_y == count_y - 1
    mask_at = 4 * levels

    @pl.when(level == 0)
    def _():
        fold = fold_ref[pl.ds(index_x, 1), :]
        total = jnp.zeros((rows, LANES), F32)
        sources = [(0, own_ref), (-1, west_ref), (1, east_ref)]
        sources += [(shift, ref) for shift, ref in zip(range(2, count_x - 1), far_refs)]
        for shift, ref in sources:
            at = lax.rem(index_x + shift + count_x, count_x)
            block = ref[...] if ref.shape[0] == rows else ref[fold_start : fold_start + rows, :]
            chosen = (iota((rows, rows), 0) + at * rows == fold).astype(F32)
            total += lax.dot_general(
                chosen, block, (((0,), (0,)), ((), ())),
                precision=lax.Precision.HIGHEST, preferred_element_type=F32,
            )
        lane = iota((rows, LANES), 1)
        flipped = jnp.logical_and(lane >= EDGE_VELOCITY * levels, lane < (EDGE_VELOCITY + 1) * levels)
        total = jnp.where(flipped, -total, total)
        turned_ref[...] = jnp.where(
            last_y, jnp.where(is_ocean, total, 0.0), north_ref[...]
        )

    pressure, zonal, meridional, tracer = (state_ref[0, v, 0] for v in range(4))
    sea = mask_ref[0].astype(F32)
    half = 0.5 * wave_ref[0, level]
    spread = spread_ref[0, level]
    drag = gains_ref[0, 2]

    def keeping(sea_values):
        first = jnp.where(level == 0, drag, 0.0)
        return jnp.where(is_ocean, sea_values, 1.0 - first * (1.0 - sea_values))

    has_west = jnp.where(jnp.logical_or(is_ocean, index_x > 0), 1.0, 0.0)
    has_east = jnp.where(jnp.logical_or(is_ocean, index_x < count_x - 1), 1.0, 0.0)
    has_south = jnp.where(index_y > 0, 1.0, 0.0)
    has_north = jnp.where(jnp.logical_or(is_ocean, jnp.logical_not(last_y)), 1.0, 0.0)

    def row_at(ref, row):
        parts = [ref[pl.ds(p * height + row, 1), :] for p in range(cols // LANES)]
        return jnp.concatenate(parts, axis=1)

    def west_row(q):
        return row_at(west_ref, q * levels + level)

    def east_row(q):
        return row_at(east_ref, q * levels + level)

    def south_col(at):
        return pltpu.roll(south_ref[...], lax.rem(LANES - at, LANES), 1)

    def north_col(at):
        return pltpu.roll(turned_ref[...], LANES - 1 - at, 1)

    row_ids = iota((rows, cols), 0)
    col_ids = iota((rows, cols), 1)

    def from_west(field, edge):
        return jnp.where(row_ids == 0, edge, pltpu.roll(field, 1, 0))

    def from_east(field, edge):
        return jnp.where(row_ids == rows - 1, edge, pltpu.roll(field, rows - 1, 0))

    def from_south(field, edge):
        wide = jnp.concatenate([edge, jnp.zeros((rows, cols - LANES), F32)], axis=1)
        return jnp.where(col_ids == 0, wide, pltpu.roll(field, 1, 1))

    def from_north(field, edge):
        wide = jnp.concatenate([jnp.zeros((rows, cols - LANES), F32), edge], axis=1)
        return jnp.where(col_ids == cols - 1, wide, pltpu.roll(field, cols - 1, 1))

    keep = keeping(sea)
    tendency = jnp.where(is_ocean, sea, 1.0)
    new_zonal = keep * (
        zonal
        - half * (
            from_east(pressure, has_east * east_row(EDGE_P))
            - from_west(pressure, has_west * west_row(EDGE_P))
        )
    )
    south_p = south_col(EDGE_P * levels + level)
    north_p = north_col(EDGE_P * levels + level)
    new_meridional = keep * (
        meridional
        - half * (from_north(pressure, has_north * north_p) - from_south(pressure, has_south * south_p))
    )
    laplace = (
        from_east(tracer, has_east * east_row(EDGE_T))
        + from_west(tracer, has_west * west_row(EDGE_T))
        + from_north(tracer, has_north * north_col(EDGE_T * levels + level))
        + from_south(tracer, has_south * south_col(EDGE_T * levels + level))
        - 4.0 * tracer
    )
    new_tracer = tracer + spread * tendency * laplace
    west_zonal = keeping(row_at(west_ref, mask_at)) * (
        west_row(EDGE_VELOCITY) - half * (pressure[0:1, :] - west_row(SECOND_P))
    )
    east_zonal = keeping(row_at(east_ref, mask_at)) * (
        east_row(EDGE_VELOCITY) - half * (east_row(SECOND_P) - pressure[rows - 1 : rows, :])
    )
    south_meridional = keeping(south_col(mask_at)) * (
        south_col(EDGE_VELOCITY * levels + level)
        - half * (pressure[:, :LANES] - south_col(SECOND_P * levels + level))
    )
    north_meridional = keeping(north_col(mask_at)) * (
        north_col(EDGE_VELOCITY * levels + level)
        - half * (north_col(SECOND_P * levels + level) - pressure[:, cols - LANES :])
    )
    divergence = (
        from_east(new_zonal, has_east * east_zonal)
        - from_west(new_zonal, has_west * west_zonal)
        + from_north(new_meridional, has_north * north_meridional)
        - from_south(new_meridional, has_south * south_meridional)
    )
    out_ref[0, 0, 0] = pressure - half * divergence
    out_ref[0, 1, 0] = new_zonal
    out_ref[0, 2, 0] = new_meridional
    out_ref[0, 3, 0] = new_tracer


def stencil(model_state, sea_mask, west, east, south, north, own, fars, fold_map, wave_speed, diffusivity, gains, sizes):
    comps, count_x, count_y = sizes
    levels, rows, cols = model_state.shape[2:]
    fold = fold_map.reshape(count_x, rows)
    whole = lambda array: pl.BlockSpec(array.shape, lambda l: (0,) * array.ndim)
    scalar = pl.BlockSpec(memory_space=pltpu.SMEM)
    own_rows = pl.BlockSpec(own.shape, lambda l: (0, 0))
    field = pl.BlockSpec((1, 4, 1, rows, cols), lambda l: (0, 0, l, 0, 0))
    return pl.pallas_call(
        functools.partial(stencil_body, levels, rows, cols, comps, count_x, count_y),
        grid=(levels,),
        in_specs=[
            field, whole(sea_mask), whole(west), whole(east), whole(south), whole(north),
            own_rows, whole(fold), scalar, scalar, scalar,
        ] + [whole(far) for far in fars],
        out_specs=field,
        out_shape=jax.ShapeDtypeStruct(model_state.shape, F32),
        scratch_shapes=[pltpu.VMEM((rows, LANES), F32)],
        compiler_params=pltpu.CompilerParams(vmem_limit_bytes=VMEM_BYTES),
    )(model_state, sea_mask, west, east, south, north, own, fold, wave_speed, diffusivity, gains, *fars)


def scatter_body(rows, cols, comps, block_count, new_ref, state_ref, mask_ref, gains_ref, *rest):
    slab_refs, out_ref = rest[:block_count], rest[block_count]
    spread_ref, column_ref, total_ref = rest[block_count + 1 :]
    here = lax.axis_index("comp")
    is_ocean = here == comps - 1
    near, channels, groups, lanes = slab_refs[0].shape
    total_ref[...] = jnp.zeros_like(total_ref)
    row_ids = iota((rows, lanes), 0)
    col_ids = iota((cols, lanes), 0)
    lane = iota((1, lanes), 1)
    for slab_ref in slab_refs:

        def one(n, carry, slab_ref=slab_ref):
            for g in range(groups):
                cells = slab_ref[n, 4, g : g + 1, :].astype(I32)
                slot = lane + g * lanes
                mine = jnp.logical_or(is_ocean, slot % (comps - 1) == here)
                row = jnp.where(mine, cells // cols, -1)
                cut = slice(g * lanes, (g + 1) * lanes)
                column_ref[:, cut] = (col_ids == cells % cols).astype(F32).astype(BF16)
                in_row = row_ids == row
                for v in range(4):
                    high, low = split_two(slab_ref[n, v, g : g + 1, :])
                    spread_ref[v * rows : (v + 1) * rows, cut] = jnp.where(
                        in_row, high.astype(F32), 0.0
                    ).astype(BF16)
                    spread_ref[(v + 4) * rows : (v + 5) * rows, cut] = jnp.where(
                        in_row, low.astype(F32), 0.0
                    ).astype(BF16)
            total_ref[...] += lax.dot_general(
                spread_ref[...], column_ref[...], (((1,), (1,)), ((), ())),
                preferred_element_type=F32,
            )
            return carry

        lax.fori_loop(0, near, one, 0)

    sea = mask_ref[0].astype(F32)
    tendency = jnp.where(is_ocean, sea, 1.0)
    sums = [
        total_ref[v * rows : (v + 1) * rows, :] + total_ref[(v + 4) * rows : (v + 5) * rows, :]
        for v in range(4)
    ]
    out_ref[0, 0, 0] = new_ref[0, 0, 0]
    for v, total, gain in ((3, sums[0], 0), (1, sums[1], 1), (2, sums[2], 1)):
        change = tendency * gains_ref[0, gain] * (total - sums[3] * state_ref[0, v, 0])
        out_ref[0, v, 0] = new_ref[0, v, 0] + change


def scatter_slots(new_state, model_state, sea_mask, gains, slabs, comps):
    rows, cols = model_state.shape[3:]
    near, channels, groups, lanes = slabs[0].shape
    whole = lambda array: pl.BlockSpec(array.shape, lambda i: (0,) * array.ndim)
    surface = pl.BlockSpec((1, 4, 1, rows, cols), lambda i: (0, 0, 0, 0, 0))
    return pl.pallas_call(
        functools.partial(scatter_body, rows, cols, comps, len(slabs)),
        grid=(1,),
        in_specs=[surface, surface, whole(sea_mask), pl.BlockSpec(memory_space=pltpu.SMEM)]
        + [whole(slab) for slab in slabs],
        out_specs=surface,
        out_shape=jax.ShapeDtypeStruct(new_state.shape, F32),
        scratch_shapes=[
            pltpu.VMEM((8 * rows, groups * lanes), BF16),
            pltpu.VMEM((cols, groups * lanes), BF16),
            pltpu.VMEM((8 * rows, cols), F32),
        ],
        input_output_aliases={0: 0},
        compiler_params=pltpu.CompilerParams(vmem_limit_bytes=VMEM_BYTES),
    )(new_state, model_state, sea_mask, gains, *slabs)


def shards(
    model_state, sea_mask, wave_speed, diffusivity, surface_gains, area_table,
    own_cells, target_cells, weight_ids, pair_counts, fold_map,
):
    comps, count_x, count_y = (lax.axis_size(a) for a in ("comp", "tx", "ty"))
    positions = count_x * count_y

    def around(block, shift):
        return lax.ppermute(block, "tx", [(i, (i + shift) % count_x) for i in range(count_x)])

    y_pair = count_y == 2
    up, down, y_block = pack_halos(model_state, sea_mask, y_pair)
    rows = model_state.shape[3]
    own_high = up[up.shape[0] - rows :]
    west = around(up, 1)
    east = around(down, -1)
    if y_pair:
        south = north = lax.ppermute(y_block, "ty", [(0, 1), (1, 0)])
    else:
        south = lax.ppermute(own_high, "ty", [(j, j + 1) for j in range(count_y - 1)])
        north = lax.ppermute(y_block, "ty", [(j + 1, j) for j in range(count_y - 1)])
    fars = []
    for shift in range(2, count_x - 1):
        pairs = []
        for i in range(count_x):
            ends = [((comps - 1) * count_x + k) * count_y + count_y - 1 for k in ((i + shift) % count_x, i)]
            pairs.append(tuple(ends))
        fars.append(lax.ppermute(own_high, ("comp", "tx", "ty"), pairs))

    slabs = gather_slots(model_state, own_cells, target_cells, weight_ids, area_table, pair_counts)
    arrived = [slabs[0]]
    for n in range(1, len(slabs)):
        offset = n % 2 + n // 2 * count_y
        arrived.append(
            lax.ppermute(slabs[n], ("tx", "ty"), [(s, (s + offset) % positions) for s in range(positions)])
        )
    arrived = jnp.stack(arrived)
    received = [
        lax.ppermute(arrived, "comp", [(g, comps - 1), (comps - 1, g)]) for g in range(comps - 1)
    ]
    new_state = stencil(
        model_state, sea_mask, west, east, south, north, own_high, fars, fold_map,
        wave_speed, diffusivity, surface_gains, (comps, count_x, count_y),
    )
    return scatter_slots(new_state, model_state, sea_mask, surface_gains, received, comps)


def solution(mesh):
    in_specs = (
        P("comp", None, None, "tx", "ty"),
        P("comp", "tx", "ty"),
        P("comp", None),
        P("comp", None),
        P("comp", None),
        P(),
        P("comp", ("tx", "ty"), None, None),
        P("comp", ("tx", "ty"), None, None),
        P("comp", ("tx", "ty"), None, None),
        P("comp", ("tx", "ty"), None),
        P(),
    )
    out_specs = P("comp", None, None, "tx", "ty")
    return jax.shard_map(shards, mesh=mesh, in_specs=in_specs, out_specs=out_specs, check_vma=False)
```

time: 833 us -> 77.1 us (0.09)
  the two profiles are of different devices: /device:TPU:3 before, /device:TPU:0 now
where the time goes in v1:
time: 77.1 us; the launch traced here: 76.6 us
  Pallas kernels  48.3 us (63%)
  starting transfers between devices  18.7 us (24%)
  waiting for transfers between devices  6.56 us (9%)
  local copies, waits for them, and re-layouts  2.84 us (4%)
    pallas_call x1, Pallas kernels, scatter_slots(): pl.pallas_call(functools.partial(scatter_body, rows, cols, comps, len(sla...  25.2 us
    pallas_call x1, Pallas kernels, stencil(): pl.pallas_call(functools.partial(stencil_body, levels, rows, cols, comps,...  8.89 us
    pallas_call x1, Pallas kernels, gather_slots(): pl.pallas_call(functools.partial(gather_body, rows, cols, slots), grid=(1...  7.88 us
    ppermute x3, starting transfers between devices, shards(): lax.ppermute(arrived, 'comp', [(g, comps - 1), (comps - 1, g)])  7.33 us
    ppermute x3, starting transfers between devices, shards(): lax.ppermute(slabs[n], ('tx', 'ty'), [(s, (s + offset) % positions) for s...  7.08 us
    ppermute x2, waiting for transfers between devices, around(): lax.ppermute(block, 'tx', [(i, (i + shift) % count_x) for i in range(coun...  6.54 us
    pallas_call x1, Pallas kernels, pack_halos(): pl.pallas_call(functools.partial(pack_body, levels, rows, cols, y_pair),...  6.38 us
    ppermute x2, starting transfers between devices, around(): lax.ppermute(block, 'tx', [(i, (i + shift) % count_x) for i in range(coun...  2.08 us
  transfers between devices with their start and end apart: 10, of which 2 were waited for; matrix products, arithmetic and copies ran while one was open for 1% of the time, Pallas kernels for 20%

profile of v1, /device:TPU:0, one launch (start us, length us, event | category | flops | bytes accessed | tf_op | source)
XLA Modules:
  0.0 76.6 jit_solution(1209258389642822733)
XLA Ops:
  0.0 7.9 %shard_map.111 = (f32[5,16,128]{2,1,0:T(8,128)}, f32[5,16,128]{2,1,0:T(8,128)}, f32[5,16,128]{2,1,0:T(8,128)}, f32[5,16,128]{2,1,0:T(8,128)}) custom-call(f32[1,4,8,128,256]{4,3,2,1,0:T(8,128)} %state_ref.7, s32[1,1,4,2048]{3,2,1,0:T(4,128)} %own_ref.1, s32[1,1,4,2048]{3,2,1,0:T(4,128)} %target_ref.1, s32[1,1,4,2048]{3,2,1,0:T(4,128)} %ids_ref.1, ...), custom_call_target="tpu_custom_call" | custom-call | tf_op jit(solution)/shard_map/pallas_call | solution.py:171
  7.9 0.0 copy-start.8
  7.9 3.0 %collective-permute-start.4 = (f32[5,16,128]{2,1,0:T(8,128)}, f32[5,16,128]{2,1,0:T(8,128)S(1)}, u32[]{:S(2)}, u32[]{:S(2)}) collective-permute-start(f32[5,16,128]{2,1,0:T(8,128)} %get-tuple-element.16), channel_id=1, source_target_pairs={{0,1},{1,2},{2,3},{3,4},{4,5},{5,6},{6,7},{7,0},{8,9},{9,10},{10,1... | collective-permute-start | bytes 122888 | tf_op jit(solution)/shard_map/ppermute | solution.py:449
  10.8 1.6 %collective-permute-start.5 = (f32[5,16,128]{2,1,0:T(8,128)}, f32[5,16,128]{2,1,0:T(8,128)S(1)}, u32[]{:S(2)}, u32[]{:S(2)}) collective-permute-start(f32[5,16,128]{2,1,0:T(8,128)} %get-tuple-element.17), channel_id=1, source_target_pairs={{0,2},{1,3},{2,4},{3,5},{4,6},{5,7},{6,0},{7,1},{8,10},{9,11},{10,... | collective-permute-start | bytes 122888 | tf_op jit(solution)/shard_map/ppermute | solution.py:449
  12.4 2.5 %collective-permute-start.6 = (f32[5,16,128]{2,1,0:T(8,128)}, f32[5,16,128]{2,1,0:T(8,128)S(1)}, u32[]{:S(2)}, u32[]{:S(2)}) collective-permute-start(f32[5,16,128]{2,1,0:T(8,128)} %get-tuple-element.18), channel_id=1, source_target_pairs={{0,3},{1,4},{2,5},{3,6},{4,7},{5,0},{6,1},{7,2},{8,11},{9,12},{10,... | collective-permute-start | bytes 122888 | tf_op jit(solution)/shard_map/ppermute | solution.py:449
  15.0 6.4 %shard_map.109 = (f32[208,128]{1,0:T(8,128)}, f32[208,128]{1,0:T(8,128)}, f32[128,128]{1,0:T(8,128)}) custom-call(f32[1,4,8,128,256]{4,3,2,1,0:T(8,128)} %state_ref.7, s32[1,128,256]{2,1,0:T(8,128)} %mask_ref.5), custom_call_target="tpu_custom_call" | custom-call | tf_op jit(solution)/shard_map/pallas_call | solution.py:104
  21.3 0.8 %slice.3.own_ref = f32[128,128]{1,0:T(8,128)S(1)} slice(f32[208,128]{1,0:T(8,128)} %get-tuple-element.12), slice={[80:208], [0:128]} | slice | bytes 131072 | tf_op jit(solution)/shard_map/slice | solution.py:428
  22.2 0.0 copy-start.1
  22.2 0.7 collective-permute-start.3
  22.9 1.6 %collective-permute-start.2 = (f32[128,128]{1,0:T(8,128)}, f32[128,128]{1,0:T(8,128)S(1)}, u32[]{:S(2)}, u32[]{:S(2)}) collective-permute-start(f32[128,128]{1,0:T(8,128)} %get-tuple-element.14), channel_id=1, source_target_pairs={{0,1},{1,0},{2,3},{3,2},{4,5},{5,4},{6,7},{7,6},{8,9},{9,8},{10,11... | collective-permute-start | bytes 196616 | tf_op jit(solution)/shard_map/ppermute | solution.py:432
  24.4 0.0 collective-permute-done.4
  24.4 0.0 collective-permute-done.5
  24.4 0.0 collective-permute-done.6
  24.4 0.0 copy-done.8
  24.5 0.7 collective-permute-start.9
  25.2 0.7 collective-permute-start.8
  25.8 6.0 %collective-permute-start.7 = (f32[4,5,16,128]{3,2,1,0:T(8,128)S(1)}, f32[4,5,16,128]{3,2,1,0:T(8,128)S(1)}, u32[]{:S(2)}, u32[]{:S(2)}) collective-permute-start(f32[4,5,16,128]{3,2,1,0:T(8,128)S(1)} %pad_maximum_fusion), channel_id=1, source_target_pairs={{0,24},{24,0},{1,25},{25,1},{2,26},{26,2},{3,27},{27,3},{4,28},{28... | collective-permute-start | bytes 491528 | tf_op jit(solution)/shard_map/ppermute | solution.py:453
  31.8 0.0 collective-permute-done.3.rest_0_
  31.8 0.0 copy-start.7
  31.9 1.9 %collective-permute-start.1 = (f32[208,128]{1,0:T(8,128)}, f32[208,128]{1,0:T(8,128)S(1)}, u32[]{:S(2)}, u32[]{:S(2)}) collective-permute-start(f32[208,128]{1,0:T(8,128)} %get-tuple-element.13), channel_id=1, source_target_pairs={{0,6},{2,0},{4,2},{6,4},{1,7},{3,1},{5,3},{7,5},{8,14},{10,8},{12,... | collective-permute-start | bytes 319496 | tf_op jit(solution)/shard_map/ppermute | solution.py:423
  33.8 0.0 collective-permute-done.2.south_ref.north_ref
  33.8 0.0 copy-start
  33.8 0.2 collective-permute-start
  33.9 2.9 %collective-permute-done.1.east_ref = f32[208,128]{1,0:T(8,128)S(1)} collective-permute-done((f32[208,128]{1,0:T(8,128)}, f32[208,128]{1,0:T(8,128)S(1)}, u32[]{:S(2)}, u32[]{:S(2)}) %collective-permute-start.1) | collective-permute-done | bytes 106528 | tf_op jit(solution)/shard_map/ppermute | solution.py:423
  36.8 0.0 copy-start.5
  36.8 3.7 %collective-permute-done.west_ref = f32[208,128]{1,0:T(8,128)S(1)} collective-permute-done((f32[208,128]{1,0:T(8,128)}, f32[208,128]{1,0:T(8,128)S(1)}, u32[]{:S(2)}, u32[]{:S(2)}) %collective-permute-start) | collective-permute-done | bytes 106528 | tf_op jit(solution)/shard_map/ppermute | solution.py:423
  40.5 0.0 copy-start.6
  40.5 0.0 copy-done.1
  40.5 0.0 copy-done.7
  40.5 0.0 copy-done
  40.5 0.0 copy-done.5
  40.5 0.6 copy-done.6
  41.1 8.9 %shard_map.110.new_ref = f32[1,4,8,128,256]{4,3,2,1,0:T(8,128)} custom-call(f32[1,4,8,128,256]{4,3,2,1,0:T(8,128)} %state_ref.7, s32[1,128,256]{2,1,0:T(8,128)} %mask_ref.5, f32[208,128]{1,0:T(8,128)} %copy-done.6, f32[208,128]{1,0:T(8,128)} %copy-done.5, f32[128,128]{1,0:T(8,128)} %copy-done, f32[128,128]{1,0:T(8,128)} %copy-done, f32[128,128]{1,0:T(8,128)} %copy-done.1, ...), custom_call_target="tpu_custom_call" | custom-call | tf_op jit(solution)/shard_map/pallas_call | solution.py:330
  50.0 0.0 collective-permute-done.9.rest_2_
  50.0 0.0 copy-start.2
  50.0 0.0 collective-permute-done.8.rest_1_
  50.0 0.0 copy-start.3
  50.1 0.0 collective-permute-done.7.rest_0_
  50.1 0.6 copy-done.2
  50.7 0.1 copy-done.3
  50.8 0.0 copy-start.4
  50.8 0.7 copy-done.4
  51.4 25.2 %shard_map.112 = f32[1,4,8,128,256]{4,3,2,1,0:T(8,128)} custom-call(f32[1,4,8,128,256]{4,3,2,1,0:T(8,128)} %shard_map.110.new_ref, f32[1,4,8,128,256]{4,3,2,1,0:T(8,128)} %state_ref.7, s32[1,128,256]{2,1,0:T(8,128)} %mask_ref.5, f32[1,3]{1,0:T(1,128)} %gains_ref.3, f32[4,5,16,128]{3,2,1,0:T(8,128)} %copy-done.4, ...), custom_call_target="tpu_custom_call", output_to_operand_aliasing={{}: (0, {})} | custom-call | tf_op jit(solution)/shard_map/pallas_call | solution.py:398
  (1 shorter events, 0.0 us)
Async XLA Ops:
  7.9 16.6 %copy-start.8 = (f32[5,16,128]{2,1,0:T(8,128)S(1)}, f32[5,16,128]{2,1,0:T(8,128)}, u32[]{:S(2)}) copy-start(f32[5,16,128]{2,1,0:T(8,128)} %get-tuple-element.15) | copy-start | bytes 122884
  7.9 16.6 %collective-permute-start.4 = (f32[5,16,128]{2,1,0:T(8,128)}, f32[5,16,128]{2,1,0:T(8,128)S(1)}, u32[]{:S(2)}, u32[]{:S(2)}) collective-permute-start(f32[5,16,128]{2,1,0:T(8,128)} %get-tuple-element.16), channel_id=1, source_target_pairs={{0,1},{1,2},{2,3},{3,4},{4,5},{5,6},{6,7},{7,0},{8,9},{9,10},{10,1... | collective-permute-start | bytes 122888 | tf_op jit(solution)/shard_map/ppermute | solution.py:449
  10.8 13.6 %collective-permute-start.5 = (f32[5,16,128]{2,1,0:T(8,128)}, f32[5,16,128]{2,1,0:T(8,128)S(1)}, u32[]{:S(2)}, u32[]{:S(2)}) collective-permute-start(f32[5,16,128]{2,1,0:T(8,128)} %get-tuple-element.17), channel_id=1, source_target_pairs={{0,2},{1,3},{2,4},{3,5},{4,6},{5,7},{6,0},{7,1},{8,10},{9,11},{10,... | collective-permute-start | bytes 122888 | tf_op jit(solution)/shard_map/ppermute | solution.py:449
  12.4 12.0 %collective-permute-start.6 = (f32[5,16,128]{2,1,0:T(8,128)}, f32[5,16,128]{2,1,0:T(8,128)S(1)}, u32[]{:S(2)}, u32[]{:S(2)}) collective-permute-start(f32[5,16,128]{2,1,0:T(8,128)} %get-tuple-element.18), channel_id=1, source_target_pairs={{0,3},{1,4},{2,5},{3,6},{4,7},{5,0},{6,1},{7,2},{8,11},{9,12},{10,... | collective-permute-start | bytes 122888 | tf_op jit(solution)/shard_map/ppermute | solution.py:449
  22.2 18.3 %copy-start.1 = (f32[128,128]{1,0:T(8,128)}, f32[128,128]{1,0:T(8,128)S(1)}, u32[]{:S(2)}) copy-start(f32[128,128]{1,0:T(8,128)S(1)} %slice.3.own_ref) | copy-start | bytes 196612
  22.2 9.6 %collective-permute-start.3 = (f32[128,128]{1,0:T(8,128)S(1)}, f32[128,128]{1,0:T(8,128)S(1)}, u32[]{:S(2)}, u32[]{:S(2)}) collective-permute-start(f32[128,128]{1,0:T(8,128)S(1)} %slice.3.own_ref), channel_id=1, source_target_pairs={{29,25},{31,27},{25,29},{27,31}} | collective-permute-start | bytes 196616 | tf_op jit(solution)/shard_map/ppermute | solution.py:442
  22.9 10.9 %collective-permute-start.2 = (f32[128,128]{1,0:T(8,128)}, f32[128,128]{1,0:T(8,128)S(1)}, u32[]{:S(2)}, u32[]{:S(2)}) collective-permute-start(f32[128,128]{1,0:T(8,128)} %get-tuple-element.14), channel_id=1, source_target_pairs={{0,1},{1,0},{2,3},{3,2},{4,5},{5,4},{6,7},{7,6},{8,9},{9,8},{10,11... | collective-permute-start | bytes 196616 | tf_op jit(solution)/shard_map/ppermute | solution.py:432
  24.5 25.5 %collective-permute-start.9 = (f32[4,5,16,128]{3,2,1,0:T(8,128)S(1)}, f32[4,5,16,128]{3,2,1,0:T(8,128)S(1)}, u32[]{:S(2)}, u32[]{:S(2)}) collective-permute-start(f32[4,5,16,128]{3,2,1,0:T(8,128)S(1)} %pad_maximum_fusion), channel_id=1, source_target_pairs={{16,24},{24,16},{17,25},{25,17},{18,26},{26,18},{19,27},{27,19},{2... | collective-permute-start | bytes 491528 | tf_op jit(solution)/shard_map/ppermute | solution.py:453
  25.2 24.9 %collective-permute-start.8 = (f32[4,5,16,128]{3,2,1,0:T(8,128)S(1)}, f32[4,5,16,128]{3,2,1,0:T(8,128)S(1)}, u32[]{:S(2)}, u32[]{:S(2)}) collective-permute-start(f32[4,5,16,128]{3,2,1,0:T(8,128)S(1)} %pad_maximum_fusion), channel_id=1, source_target_pairs={{8,24},{24,8},{9,25},{25,9},{10,26},{26,10},{11,27},{27,11},{12,28... | collective-permute-start | bytes 491528 | tf_op jit(solution)/shard_map/ppermute | solution.py:453
  25.8 24.2 %collective-permute-start.7 = (f32[4,5,16,128]{3,2,1,0:T(8,128)S(1)}, f32[4,5,16,128]{3,2,1,0:T(8,128)S(1)}, u32[]{:S(2)}, u32[]{:S(2)}) collective-permute-start(f32[4,5,16,128]{3,2,1,0:T(8,128)S(1)} %pad_maximum_fusion), channel_id=1, source_target_pairs={{0,24},{24,0},{1,25},{25,1},{2,26},{26,2},{3,27},{27,3},{4,28},{28... | collective-permute-start | bytes 491528 | tf_op jit(solution)/shard_map/ppermute | solution.py:453
  31.8 8.6 %copy-start.7 = (f32[128,128]{1,0:T(8,128)}, f32[128,128]{1,0:T(8,128)S(1)}, u32[]{:S(2)}) copy-start(f32[128,128]{1,0:T(8,128)S(1)} %collective-permute-done.3.rest_0_) | copy-start | bytes 196612
  31.9 5.0 %collective-permute-start.1 = (f32[208,128]{1,0:T(8,128)}, f32[208,128]{1,0:T(8,128)S(1)}, u32[]{:S(2)}, u32[]{:S(2)}) collective-permute-start(f32[208,128]{1,0:T(8,128)} %get-tuple-element.13), channel_id=1, source_target_pairs={{0,6},{2,0},{4,2},{6,4},{1,7},{3,1},{5,3},{7,5},{8,14},{10,8},{12,... | collective-permute-start | bytes 319496 | tf_op jit(solution)/shard_map/ppermute | solution.py:423
  33.8 6.7 %copy-start = (f32[128,128]{1,0:T(8,128)}, f32[128,128]{1,0:T(8,128)S(1)}, u32[]{:S(2)}) copy-start(f32[128,128]{1,0:T(8,128)S(1)} %collective-permute-done.2.south_ref.north_ref) | copy-start | bytes 196612
  33.8 6.7 %collective-permute-start = (f32[208,128]{1,0:T(8,128)}, f32[208,128]{1,0:T(8,128)S(1)}, u32[]{:S(2)}, u32[]{:S(2)}) collective-permute-start(f32[208,128]{1,0:T(8,128)} %get-tuple-element.12), channel_id=1, source_target_pairs={{0,2},{2,4},{4,6},{6,0},{1,3},{3,5},{5,7},{7,1},{8,10},{10,12},{12... | collective-permute-start | bytes 319496 | tf_op jit(solution)/shard_map/ppermute | solution.py:423
  36.8 3.7 %copy-start.5 = (f32[208,128]{1,0:T(8,128)}, f32[208,128]{1,0:T(8,128)S(1)}, u32[]{:S(2)}) copy-start(f32[208,128]{1,0:T(8,128)S(1)} %collective-permute-done.1.east_ref) | copy-start | bytes 319492
  40.5 0.6 copy-start.6
  50.0 0.7 copy-start.2
  50.0 0.7 copy-start.3
  50.8 0.7 copy-start.4
